TPU v7x, 32 devices: a whole 2x2x4 slice. The times are simulated.
32 devices in a mesh: grp: 2 (over y), seq: 4 (over z), blk: 2 (over x), rep: 2 (over core).
Axes of the slice: x: 2, y: 2, z: 4, core: 2. Of those that a mesh axis runs over, the one named last changes fastest.
Arguments:
- q_proj: bfloat16 [8, 2048, 512], P(('grp', 'blk', 'rep'), 'seq'), parts along dimension 0, may hold values from -6 to 6
- k_proj: bfloat16 [8, 2048, 128], P(('grp', 'blk', 'rep'), 'seq'), parts along dimension 0, may hold values from -6 to 6
- v_proj: bfloat16 [8, 2048, 128], P(('grp', 'blk', 'rep'), 'seq'), parts along dimension 0, may hold values from -6 to 6
- q_gain: float32 [128], replicated, may hold values from 0.5 to 1.5
- k_gain: float32 [128], replicated, may hold values from 0.5 to 1.5
- out_weight: bfloat16 [512, 2560], P('seq'), may hold values from -0.25 to 0.25
- lengths: int32 [8, 1], P(('grp', 'blk', 'rep')), parts along dimension 0, may hold values from 512 to 2048, as said below
- query_emb: bfloat16 [512, 2560], P(('grp', 'blk')), parts along dimension 0, may hold values from -6 to 6
- teacher: float32 [512, 4], P(('grp', 'blk')), parts along dimension 0, may hold values from -16 to 16
Outputs:
- q_grad: bfloat16 [8, 2048, 512], P(('grp', 'blk', 'rep'), 'seq'), parts along dimension 0
- k_grad: bfloat16 [8, 2048, 128], P(('grp', 'blk', 'rep'), 'seq'), parts along dimension 0
- v_grad: bfloat16 [8, 2048, 128], P(('grp', 'blk', 'rep'), 'seq'), parts along dimension 0
- weight_grad: bfloat16 [1024, 2560], P(('grp', 'seq')), parts along dimension 0
- row_loss: float32 [512], P(('grp', 'blk')), parts along dimension 0
- col_loss: float32 [8], P('grp'), parts along dimension 0
There are 2 independent parts, one for each index of `grp`. A program takes and returns all parts, laid end to end along the dimension named above; an argument that names none is the same for every part. Nothing has to cross between parts.
Inputs may be any that keep to these rules, and one draw needn't show every extreme that they name: `lengths`: live tokens of each passage, counted from its first position; the rest is padding.
All inputs are finite; a program needn't handle non-finite values.
Results may differ from a plain program's by a relative error of at most 0.017.
Values may be sent and summed in bfloat16 or wider, within the bound.
A program may use at most 64 MiB of HBM per device.

v0:
```python
import math
import jax
import jax.numpy as jnp
from jax import lax
from jax.sharding import PartitionSpec as P

HD = 128
PASS_LEN = 2048
logit_divisor = 0.05


def rms_scale(wide):
    return lax.rsqrt(jnp.mean(wide * wide, axis=-1, keepdims=True) + 1e-06)


def normed(source, gain_weights):
    wide = source.astype(jnp.float32)
    return (wide * rms_scale(wide) * gain_weights).astype(jnp.bfloat16)


def norm_back(source, gain_weights, grad_out):
    wide = source.astype(jnp.float32)
    inv_rms = rms_scale(wide)
    scaled_grad = gain_weights * grad_out
    return (
        inv_rms * scaled_grad
        - wide * inv_rms**3 * jnp.mean(scaled_grad * wide, axis=-1, keepdims=True)
    ).astype(jnp.bfloat16)


def shards(q_proj, k_proj, v_proj, q_gain, k_gain, out_weight, lengths, query_emb, teacher):
    number_of_sequences = lax.axis_size("seq")
    blk_count = lax.axis_size("blk")
    tok_dev = q_proj.shape[1]
    heads_all = q_proj.shape[2] // HD
    kv_heads = k_proj.shape[2] // HD
    group_size = heads_all // kv_heads
    local_heads = out_weight.shape[0] // HD
    group_tok = tok_dev * number_of_sequences
    passes = group_tok // PASS_LEN
    pass_lens = lengths[0]
    inv_root = 1.0 / math.sqrt(HD)
    block_rows = min(512, PASS_LEN)
    block_count = PASS_LEN // block_rows

    def widen(rows):
        spread = jnp.broadcast_to(
            rows.reshape(tok_dev, kv_heads, 1, HD), (tok_dev, kv_heads, group_size, HD)
        )
        return spread.reshape(tok_dev, heads_all * HD)

    q_heads, k_heads, v_heads = (
        lax.all_to_all(q_proj[0], "seq", split_axis=1, concat_axis=0, tiled=True),
        lax.all_to_all(widen(k_proj[0]), "seq", split_axis=1, concat_axis=0, tiled=True),
        lax.all_to_all(widen(v_proj[0]), "seq", split_axis=1, concat_axis=0, tiled=True),
    )
    head_shape = (passes, PASS_LEN, local_heads, HD)
    q_raw = q_heads.reshape(head_shape)
    k_raw = k_heads.reshape(head_shape)
    v_all = v_heads.reshape(head_shape)
    q_unit = normed(q_raw, q_gain)
    k_unit = normed(k_raw, k_gain)
    positions = lax.iota(jnp.int32, PASS_LEN)
    passage = 0
    q_block = q_unit[passage]
    k_block = k_unit[passage]
    stored = []
    for attend_index in range(block_count):
        attend_ending = (attend_index + 1) * block_rows
        rows_here = q_block[attend_index * block_rows : attend_ending]
        logits = (
            jnp.einsum(
                "thd,uhd->htu",
                rows_here,
                k_block[:attend_ending],
                preferred_element_type=jnp.float32,
            )
            * inv_root
        )
        causal = (attend_index * block_rows + lax.iota(jnp.int32, block_rows))[:, None] >= lax.iota(
            jnp.int32, attend_ending
        )[None, :]
        powers = jnp.where(causal[None], jnp.exp(logits), 0.0)
        stored.append(
            lax.optimization_barrier(
                (powers / jnp.sum(powers, axis=2, keepdims=True)).astype(jnp.bfloat16)
            )
        )
    blocks = stored
    saved_blocks = [blocks]
    live_len = pass_lens[passage]
    live_mask = (positions < live_len).astype(jnp.bfloat16)
    col_weight = jnp.zeros((local_heads, PASS_LEN), jnp.float32)
    for index in range(block_count):
        ending = (index + 1) * block_rows
        column_part = jnp.einsum(
            "t,htu->hu",
            live_mask[index * block_rows : ending],
            blocks[index],
            preferred_element_type=jnp.float32,
        )
        col_weight = col_weight.at[:, :ending].add(column_part)
    col_weight = col_weight / live_len.astype(jnp.float32)
    pooled_list = [jnp.sum(col_weight.T[:, :, None] * v_all[passage].astype(jnp.float32), axis=0)]
    weight_list = [col_weight.astype(jnp.bfloat16)]
    pooled = jnp.stack(pooled_list)
    col_weights = jnp.stack(weight_list)
    pooled_flat = pooled.reshape(passes, local_heads * HD).astype(jnp.bfloat16)
    partial_value = jnp.dot(pooled_flat, out_weight, preferred_element_type=jnp.float32)
    summed = lax.psum(partial_value, "seq")
    inv_norm = lax.rsqrt(jnp.sum(summed * summed, axis=1, keepdims=True) + 1e-06)
    passage_unit = summed * inv_norm
    passage_all = lax.all_gather(
        passage_unit.astype(jnp.bfloat16), ("blk", "rep"), axis=0, tiled=True
    )
    query_wide = query_emb.astype(jnp.float32)
    request_unit_length = (
        query_wide * lax.rsqrt(jnp.sum(query_wide * query_wide, axis=1, keepdims=True) + 1e-06)
    ).astype(jnp.bfloat16)
    learner_similarities = (
        lax.dot_general(
            request_unit_length,
            passage_all,
            (((1,), (1,)), ((), ())),
            preferred_element_type=jnp.float32,
        )
        / logit_divisor
    )
    exp_student = jnp.exp(learner_similarities)
    exp_teacher = jnp.exp(teacher)
    row_student = jnp.sum(exp_student, axis=1, keepdims=True)
    row_teacher = jnp.sum(exp_teacher, axis=1, keepdims=True)
    gap = exp_teacher * (teacher - learner_similarities)
    col_student, col_teacher, col_gap = lax.psum(
        (jnp.sum(exp_student, axis=0), jnp.sum(exp_teacher, axis=0), jnp.sum(gap, axis=0)), "blk"
    )
    row_loss = (
        jnp.sum(gap, axis=1) / row_teacher[:, 0]
        - jnp.log(row_teacher[:, 0])
        + jnp.log(row_student[:, 0])
    )
    col_loss = col_gap / col_teacher - jnp.log(col_teacher) + jnp.log(col_student)
    query_total = query_emb.shape[0] * blk_count
    passage_total = teacher.shape[1]
    similarity_derivative = (
        (exp_student / row_student - exp_teacher / row_teacher) / query_total
        + (exp_student / col_student - exp_teacher / col_teacher) / passage_total
    ).astype(jnp.bfloat16)
    grad_block = lax.psum_scatter(
        (
            lax.dot_general(
                similarity_derivative,
                request_unit_length,
                (((0,), (0,)), ((), ())),
                preferred_element_type=jnp.float32,
            )
            / logit_divisor
        ).astype(jnp.bfloat16),
        "blk",
        scatter_dimension=0,
        tiled=True,
    ).astype(jnp.float32)
    representation_derivative = lax.dynamic_slice_in_dim(
        grad_block, lax.axis_index("rep") * passes, passes, 0
    )
    grad_sum = (
        (
            representation_derivative
            - passage_unit
            * jnp.sum(passage_unit * representation_derivative, axis=1, keepdims=True)
        )
        * inv_norm
    ).astype(jnp.bfloat16)
    pooled_every, grads_every = (
        lax.all_gather(pooled_flat, ("blk", "rep"), axis=0, tiled=True),
        lax.all_gather(grad_sum, ("blk", "rep"), axis=0, tiled=True),
    )
    weight_grad = lax.dot_general(
        pooled_every, grads_every, (((0,), (0,)), ((), ())), preferred_element_type=jnp.float32
    ).astype(jnp.bfloat16)
    grad_pool = lax.dot_general(
        grad_sum, out_weight, (((1,), (1,)), ((), ())), preferred_element_type=jnp.float32
    )
    pool_heads = grad_pool.reshape(passes, local_heads, HD)
    passage = 0
    blocks = saved_blocks[passage]
    q_block = q_unit[passage]
    k_block = k_unit[passage]
    live_len = pass_lens[passage]
    live_mask = (positions < live_len).astype(jnp.float32) / live_len.astype(jnp.float32)
    value_dot = jnp.sum(v_all[passage].astype(jnp.float32) * pool_heads[passage][None], axis=2).T
    grad_k_copy = jnp.zeros((PASS_LEN, local_heads, HD), jnp.float32)
    query_parts = []
    for index in range(block_count):
        ending = (index + 1) * block_rows
        stored_block = blocks[index]
        value_here = value_dot[:, None, :ending]
        mean_dot = jnp.sum(stored_block.astype(jnp.float32) * value_here, axis=2)
        local_live_mask = live_mask[index * block_rows : ending]
        grad_logits = (
            stored_block.astype(jnp.float32)
            * local_live_mask[None, :, None]
            * (value_here - mean_dot[:, :, None])
            * inv_root
        ).astype(jnp.bfloat16)
        query_parts.append(
            jnp.einsum(
                "htu,uhd->thd", grad_logits, k_block[:ending], preferred_element_type=jnp.float32
            )
        )
        key_part = jnp.einsum(
            "htu,thd->uhd",
            grad_logits,
            q_block[index * block_rows : ending],
            preferred_element_type=jnp.float32,
        )
        grad_k_copy = grad_k_copy.at[:ending].add(key_part)
    grad_q_unit = jnp.concatenate(query_parts, axis=0)
    q_list = [norm_back(q_raw[passage], q_gain, grad_q_unit)]
    k_list = [norm_back(k_raw[passage], k_gain, grad_k_copy)]
    q_terms = jnp.stack(q_list)
    k_terms = jnp.stack(k_list)
    flat_shape = (group_tok, local_heads * HD)

    def narrow(terms):
        wide = terms.astype(jnp.float32).reshape(tok_dev, kv_heads, group_size, HD)
        return jnp.sum(wide, axis=2).astype(jnp.bfloat16).reshape(tok_dev, kv_heads * HD)

    q_back, k_back, v_back = (
        lax.all_to_all(q_terms.reshape(flat_shape), "seq", split_axis=0, concat_axis=1, tiled=True),
        lax.all_to_all(k_terms.reshape(flat_shape), "seq", split_axis=0, concat_axis=1, tiled=True),
        lax.all_to_all(
            (col_weights.astype(jnp.float32).transpose(0, 2, 1)[..., None] * pool_heads[:, None])
            .astype(jnp.bfloat16)
            .reshape(flat_shape),
            "seq",
            split_axis=0,
            concat_axis=1,
            tiled=True,
        ),
    )
    k_out = narrow(k_back)
    v_out = narrow(v_back)
    return (q_back[None], k_out[None], v_out[None], weight_grad, row_loss, col_loss)


def solution(mesh):
    placed = (
        P(("grp", "blk", "rep"), "seq", None),
        P(("grp", "blk", "rep"), "seq", None),
        P(("grp", "blk", "rep"), "seq", None),
        P(),
        P(),
        P("seq", None),
        P(("grp", "blk", "rep"), None),
        P(("grp", "blk"), None),
        P(("grp", "blk"), None),
    )
    return jax.shard_map(
        shards,
        mesh=mesh,
        in_specs=placed,
        out_specs=(
            P(("grp", "blk", "rep"), "seq", None),
            P(("grp", "blk", "rep"), "seq", None),
            P(("grp", "blk", "rep"), "seq", None),
            P(("grp", "seq"), None),
            P(("grp", "blk")),
            P("grp"),
        ),
        check_vma=False,
    )
```

profile of v0, /device:TPU:0, one launch (start us, length us, event | category | flops | bytes accessed | tf_op | source)
XLA Modules:
  0.0 180.6 jit_solution(1321558911935933446)
XLA Ops:
  0.7 1.1 copy.44
  1.8 0.8 broadcast_in_dim.25
  2.7 6.3 %all-to-all-start.1 = ((bf16[512,4,128]{0,2,1:T(8,128)(2,1)}), bf16[512,4,128]{0,2,1:T(8,128)(2,1)S(1)}, u32[]{:S(2)}, u32[]{:S(2)}) async-start(bf16[512,4,128]{0,2,1:T(8,128)(2,1)} %broadcast_in_dim.25), calls=%async_computation.1 | async-start | bytes 1048576 | tf_op jit(solution)/shard_map/all_to_all | solution.py:54
  9.0 1.0 copy.42
  10.7 12.7 %all-to-all-done.1 = bf16[512,4,128]{0,2,1:T(8,128)(2,1)S(1)} async-done(((bf16[512,4,128]{0,2,1:T(8,128)(2,1)}), bf16[512,4,128]{0,2,1:T(8,128)(2,1)S(1)}, u32[]{:S(2)}, u32[]{:S(2)}) %all-to-all-start.1) | async-done | bytes 524320 | tf_op jit(solution)/shard_map/all_to_all | solution.py:54
  23.5 3.5 %all-to-all-start = ((bf16[512,4,128]{0,2,1:T(8,128)(2,1)}), bf16[512,4,128]{0,2,1:T(8,128)(2,1)S(1)}, u32[]{:S(2)}, u32[]{:S(2)}) async-start(bf16[512,4,128]{0,2,1:T(8,128)(2,1)} %bitcast), calls=%async_computation | async-start | bytes 1048576 | tf_op jit(solution)/shard_map/all_to_all | solution.py:53
  31.1 9.8 %all-to-all-done = bf16[512,4,128]{0,2,1:T(8,128)(2,1)S(1)} async-done(((bf16[512,4,128]{0,2,1:T(8,128)(2,1)}), bf16[512,4,128]{0,2,1:T(8,128)(2,1)S(1)}, u32[]{:S(2)}, u32[]{:S(2)}) %all-to-all-start) | async-done | bytes 524320 | tf_op jit(solution)/shard_map/all_to_all | solution.py:53
  40.9 0.9 broadcast_in_dim.29
  41.8 4.3 %all-to-all-start.2 = ((bf16[512,4,128]{2,0,1:T(8,128)(2,1)}), bf16[512,4,128]{2,0,1:T(8,128)(2,1)}, u32[]{:S(2)}, u32[]{:S(2)}) async-start(bf16[512,4,128]{2,0,1:T(8,128)(2,1)} %broadcast_in_dim.29), calls=%async_computation.2 | async-start | bytes 1048576 | tf_op jit(solution)/shard_map/all_to_all | solution.py:55
  47.9 1.4 fusion.96
  52.5 1.0 fusion.99
  54.9 0.9 fusion.35
  55.8 1.0 fusion.16
  56.8 1.0 convert_reduce_fusion
  57.8 2.3 %all-to-all-done.2 = bf16[512,4,128]{2,0,1:T(8,128)(2,1)} async-done(((bf16[512,4,128]{2,0,1:T(8,128)(2,1)}), bf16[512,4,128]{2,0,1:T(8,128)(2,1)}, u32[]{:S(2)}, u32[]{:S(2)}) %all-to-all-start.2) | async-done | bytes 524320 | tf_op jit(solution)/shard_map/all_to_all | solution.py:55
  60.1 1.1 convert_element_type.407
  61.2 1.0 copy-done.11
  63.3 16.8 %psum.28 = f32[1,2560]{1,0:T(1,128)S(1)} all-reduce(f32[1,2560]{1,0:T(1,128)S(1)} %fusion.77), channel_id=1, replica_groups=mesh['grp'=2,'seq'=4,'blk'=2,'rep'=2] {'seq'}, use_global_device_ids=true, to_apply=%region_11.12 | all-reduce | flops 2560 | bytes 20480 | tf_op jit(solution)/shard_map/psum | solution.py:110
  81.4 5.2 %all-gather.1 = bf16[4,1,2560]{2,1,0:T(2,128)(2,1)S(1)} all-gather(bf16[1,1,2560]{2,1,0:T(2,128)(2,1)S(1)} %convert_bitcast_fusion.1), channel_id=1, replica_groups=mesh['grp'=2,'seq'=4,'blk'=2,'rep'=2] {'blk','rep'}, dimensions={0}, use_global_device_ids=true | all-gather | bytes 25600 | tf_op jit(solution)/shard_map/all_gather | solution.py:113
  86.6 2.0 %fusion.80 = (f32[4]{0:T(128)S(1)}, f32[128]{0:T(128)}, f32[4]{0:T(128)S(1)}, f32[128]{0:T(128)S(1)}, f32[4]{0:T(128)S(1)}, /*index=5*/f32[128]{0:T(128)S(1)}, f32[128,4]{0,1:T(4,128)S(1)}) fusion(f32[128,4]{0,1:T(4,128)S(1)} %copy-done.55, bf16[4,1,2560]{2,1,0:T(2,128)(2,1)S(1)} %all-gather.1, bf16[128,2560]{1,0:T(8,128)(2,1)} %param.36, ...), kind=kOutput, calls=%fused_computation.165 | convolution fusion | flops 3608692 | bytes 682032 | tf_op jit(solution)/shard_map/dot_general | solution.py:121
  88.6 5.4 %all-reduce.3 = (f32[4]{0:T(128)S(1)}, f32[4]{0:T(128)S(1)}, f32[4]{0:T(128)}) all-reduce(f32[4]{0:T(128)S(1)} %get-tuple-element.140, f32[4]{0:T(128)S(1)} %get-tuple-element.138, f32[4]{0:T(128)S(1)} %get-tuple-element.136), channel_id=1, replica_groups=mesh['grp'=2,'seq'=4,'blk'=2,'rep'=2] {'blk'}, use_global_device_ids=true, to_apply=%region_18.19 | all-reduce | flops 12 | bytes 96 | tf_op jit(solution)/shard_map/psum | solution.py:134
  94.1 1.4 fusion.4
  95.5 8.3 %all-reduce.2 = bf16[4,2560]{1,0:T(4,128)(2,1)S(1)} all-reduce(bf16[4,2560]{1,0:T(4,128)(2,1)S(1)} %fusion.4), channel_id=3, replica_groups=mesh['grp'=2,'seq'=4,'blk'=2,'rep'=2] {'blk'}, use_global_device_ids=true, to_apply=%region_19.20.clone | all-reduce | flops 10240 | bytes 40960
  105.9 1.6 fusion.44
  108.6 2.1 %convolution_bitcast_fusion.3 = f32[512,1,128]{0,2,1:T(8,128)} fusion(bf16[1,2048,1,128]{3,1,2,0:T(8,128)(2,1)} %copy-done.19, bf16[1,512,512]{1,2,0:T(8,128)(2,1)S(1)} %fusion.55, f32[512]{0:T(512)S(1)} %fusion.39, f32[512]{0:T(512)S(1)} %bitcast.270, f32[512]{0:T(512)S(1)} %get-tuple-element.148), kind=kOutput, calls=%fused_computation.61 | convolution fusion | flops 68681728 | bytes 923648 | tf_op jit(solution)/shard_map/htu,thd->uhd/dot_general | solution.py:211
  112.0 1.3 fusion.87
  113.3 0.9 copy-done.8
  114.9 0.9 fusion.56
  117.3 1.1 pad_maximum_fusion
  118.4 2.5 %copy.54 = f32[2048,128]{1,0:T(8,128)} copy(f32[2048,128]{0,1:T(8,128)} %pad_maximum_fusion) | data formatting | bytes 2097152 | tf_op jit(solution)/shard_map/concatenate | solution.py:218
  120.9 1.3 copy.55
  122.3 1.6 fusion.42
  123.9 2.9 %fusion.49 = bf16[4,512,128]{2,1,0:T(8,128)(2,1)} fusion(f32[4,512,128]{2,1,0:T(8,128)} %bitcast.241, bf16[512,4,128]{2,0,1:T(8,128)(2,1)} %copy-done.15, f32[4,512]{1,0:T(4,128)S(1)} %div.160, f32[4,512]{1,0:T(4,128)} %get-tuple-element.147, f32[128]{0:T(128)} %param.32, f32[4,512]{1,0:T(4,128)} %get-tuple-element.145), kind=kLoop, calls=%fused_computation.86 | loop fusion | flops 1835008 | bytes 2122240 | tf_op jit(solution)/shard_map/convert_element_type | solution.py:28
  126.8 2.1 %copy.48 = bf16[4,512,128]{1,2,0:T(8,128)(2,1)} copy(bf16[4,512,128]{2,1,0:T(8,128)(2,1)} %fusion.49) | data formatting | bytes 1048576 | tf_op jit(solution)/shard_map/convert_element_type | solution.py:28
  128.9 4.1 %all-to-all-start.3 = ((bf16[4,512,128]{1,2,0:T(8,128)(2,1)}), bf16[4,512,128]{1,2,0:T(8,128)(2,1)}, u32[]{:S(2)}, u32[]{:S(2)}) async-start(bf16[4,512,128]{1,2,0:T(8,128)(2,1)} %copy.48), calls=%async_computation.3 | async-start | bytes 1048576 | tf_op jit(solution)/shard_map/all_to_all | solution.py:230
  133.1 1.3 copy.56
  134.5 2.0 %fusion.33 = f32[2048,1,128]{0,2,1:T(8,128)S(1)} fusion(f32[2048,1,128]{0,2,1:T(8,128)S(1)} %scatter-add.25, bf16[1,2048,1,128]{3,1,2,0:T(8,128)(2,1)} %copy-done.19, bf16[1,512,1024]{2,1,0:T(8,128)(2,1)} %copy-done.12, f32[512]{0:T(512)} %copy-done.41, f32[1024]{0:T(1024)} %bitcast.267, f32[512]{0:T(512)} %get-tuple-element.151), kind=kOutput, calls=%fused_computation.60 | convolution fusion | flops 137494528 | bytes 2236416 | tf_op jit(solution)/shard_map/htu,thd->uhd/dot_general | solution.py:211
  136.5 0.9 fusion.12
  139.6 0.9 copy.50
  140.5 4.7 %all-to-all-done.3 = bf16[4,512,128]{1,2,0:T(8,128)(2,1)} async-done(((bf16[4,512,128]{1,2,0:T(8,128)(2,1)}), bf16[4,512,128]{1,2,0:T(8,128)(2,1)}, u32[]{:S(2)}, u32[]{:S(2)}) %all-to-all-start.3) | async-done | bytes 524320 | tf_op jit(solution)/shard_map/all_to_all | solution.py:230
  145.2 3.5 %all-to-all-start.4 = ((bf16[4,512,128]{1,2,0:T(8,128)(2,1)}), bf16[4,512,128]{1,2,0:T(8,128)(2,1)S(1)}, u32[]{:S(2)}, u32[]{:S(2)}) async-start(bf16[4,512,128]{1,2,0:T(8,128)(2,1)} %copy.50), calls=%async_computation.4 | async-start | bytes 1048576 | tf_op jit(solution)/shard_map/all_to_all | solution.py:231
  148.7 1.1 multiply_convert_fusion
  149.8 11.1 %all-to-all-done.4 = bf16[4,512,128]{1,2,0:T(8,128)(2,1)S(1)} async-done(((bf16[4,512,128]{1,2,0:T(8,128)(2,1)}), bf16[4,512,128]{1,2,0:T(8,128)(2,1)S(1)}, u32[]{:S(2)}, u32[]{:S(2)}) %all-to-all-start.4) | async-done | bytes 524320 | tf_op jit(solution)/shard_map/all_to_all | solution.py:231
  160.9 3.5 %all-to-all-start.5 = ((bf16[4,512,128]{2,1,0:T(8,128)(2,1)}), bf16[4,512,128]{2,1,0:T(8,128)(2,1)S(1)}, u32[]{:S(2)}, u32[]{:S(2)}) async-start(bf16[4,512,128]{2,1,0:T(8,128)(2,1)} %multiply_convert_fusion), calls=%async_computation.5 | async-start | bytes 1048576 | tf_op jit(solution)/shard_map/all_to_all | solution.py:232
  164.4 5.0 %all-gather.2 = bf16[4,1,128]{2,1,0:T(2,128)(2,1)S(1)} all-gather(bf16[1,1,128]{2,1,0:T(2,128)(2,1)S(1)} %bitcast.273), channel_id=2, replica_groups=mesh['grp'=2,'seq'=4,'blk'=2,'rep'=2] {'blk','rep'}, dimensions={0}, use_global_device_ids=true | all-gather | bytes 1280 | tf_op jit(solution)/shard_map/all_gather | solution.py:175
  169.4 5.2 %all-gather.3 = bf16[4,1,2560]{2,1,0:T(2,128)(2,1)S(1)} all-gather(bf16[1,1,2560]{2,1,0:T(2,128)(2,1)S(1)} %bitcast.262), channel_id=1, replica_groups=mesh['grp'=2,'seq'=4,'blk'=2,'rep'=2] {'blk','rep'}, dimensions={0}, use_global_device_ids=true | all-gather | bytes 25600 | tf_op jit(solution)/shard_map/all_gather | solution.py:176
  175.7 1.2 convolution_convert_fusion
  176.9 2.0 %copy.52 = bf16[1,512,512]{2,1,0:T(8,128)(2,1)} copy(bf16[1,512,512]{1,2,0:T(8,128)(2,1)} %bitcast.63) | data formatting | bytes 1048576
  (181 shorter events, 22.8 us)
Async XLA Ops:
  0.6 62.5 %copy-start = (bf16[128,2560]{1,0:T(8,128)(2,1)S(1)}, bf16[128,2560]{1,0:T(8,128)(2,1)}, u32[]{:S(2)}) copy-start(bf16[128,2560]{1,0:T(8,128)(2,1)} %param.34) | copy-start | bytes 1966084
  0.6 26.4 %copy-start.56 = (u32[32]{0:T(128)S(1)}, u32[32]{0:T(128)}, u32[]{:S(2)}) copy-start(u32[32]{0:T(128)} %constant.272) | copy-start | bytes 388
  0.7 8.3 %copy-start.22 = (bf16[1,512,512]{2,1,0:T(8,128)(2,1)S(1)}, bf16[1,512,512]{2,1,0:T(8,128)(2,1)}, u32[]{:S(2)}) copy-start(bf16[1,512,512]{2,1,0:T(8,128)(2,1)} %param.29) | copy-start | bytes 1572868
  0.7 28.9 %copy-start.21 = (bf16[128,2560]{1,0:T(8,128)(2,1)S(1)}, bf16[128,2560]{1,0:T(8,128)(2,1)}, u32[]{:S(2)}) copy-start(bf16[128,2560]{1,0:T(8,128)(2,1)} %param.36) | copy-start | bytes 1966084
  2.7 20.8 %all-to-all-start.1 = ((bf16[512,4,128]{0,2,1:T(8,128)(2,1)}), bf16[512,4,128]{0,2,1:T(8,128)(2,1)S(1)}, u32[]{:S(2)}, u32[]{:S(2)}) async-start(bf16[512,4,128]{0,2,1:T(8,128)(2,1)} %broadcast_in_dim.25), calls=%async_computation.1 | async-start | bytes 1048576 | tf_op jit(solution)/shard_map/all_to_all | solution.py:54
  23.5 17.4 %all-to-all-start = ((bf16[512,4,128]{0,2,1:T(8,128)(2,1)}), bf16[512,4,128]{0,2,1:T(8,128)(2,1)S(1)}, u32[]{:S(2)}, u32[]{:S(2)}) async-start(bf16[512,4,128]{0,2,1:T(8,128)(2,1)} %bitcast), calls=%async_computation | async-start | bytes 1048576 | tf_op jit(solution)/shard_map/all_to_all | solution.py:53
  26.9 14.0 %copy-start.26 = (bf16[1,512,128]{2,1,0:T(8,128)(2,1)S(1)}, bf16[1,512,128]{2,1,0:T(8,128)(2,1)}, u32[]{:S(2)}) copy-start(bf16[1,512,128]{2,1,0:T(8,128)(2,1)} %param.31) | copy-start | bytes 393220
  30.7 17.1 %copy-start.3 = (f32[512,4,128]{2,0,1:T(8,128)}, f32[512,4,128]{2,0,1:T(8,128)S(1)}, u32[]{:S(2)}) copy-start(f32[512,4,128]{2,0,1:T(8,128)S(1)} %convert_element_type.405) | copy-start | bytes 3145732
  41.8 5.8 %copy-start.31 = (f32[128]{0:T(128)S(1)}, f32[128]{0:T(128)}, u32[]{:S(2)}) copy-start(f32[128]{0:T(128)} %param.32) | copy-start | bytes 1540
  41.8 18.3 %all-to-all-start.2 = ((bf16[512,4,128]{2,0,1:T(8,128)(2,1)}), bf16[512,4,128]{2,0,1:T(8,128)(2,1)}, u32[]{:S(2)}, u32[]{:S(2)}) async-start(bf16[512,4,128]{2,0,1:T(8,128)(2,1)} %broadcast_in_dim.29), calls=%async_computation.2 | async-start | bytes 1048576 | tf_op jit(solution)/shard_map/all_to_all | solution.py:55
  46.3 3.0 %copy-start.15 = (bf16[512,4,128]{2,0,1:T(8,128)(2,1)}, bf16[512,4,128]{2,0,1:T(8,128)(2,1)S(1)}, u32[]{:S(2)}) copy-start(bf16[512,4,128]{2,0,1:T(8,128)(2,1)S(1)} %copy.43) | copy-start | bytes 1572868
  47.9 4.5 %copy-start.19 = (bf16[1,2048,1,128]{3,1,2,0:T(8,128)(2,1)}, bf16[1,2048,1,128]{3,1,2,0:T(8,128)(2,1)S(1)}, u32[]{:S(2)}) copy-start(bf16[1,2048,1,128]{3,1,2,0:T(8,128)(2,1)S(1)} %multiply_convert_fusion.2) | copy-start | bytes 1572868
  52.4 2.4 %copy-start.12 = (bf16[1,512,1024]{2,1,0:T(8,128)(2,1)}, bf16[1,512,1024]{2,1,0:T(8,128)(2,1)S(1)}, u32[]{:S(2)}) copy-start(bf16[1,512,1024]{2,1,0:T(8,128)(2,1)S(1)} %fusion.50) | copy-start | bytes 3145732
  53.9 1.9 %copy-start.7 = (bf16[1,512,1536]{2,1,0:T(8,128)(2,1)}, bf16[1,512,1536]{2,1,0:T(8,128)(2,1)S(1)}, u32[]{:S(2)}) copy-start(bf16[1,512,1536]{2,1,0:T(8,128)(2,1)S(1)} %fusion.27) | copy-start | bytes 4718596
  57.8 28.9 %copy-start.55 = (f32[128,4]{0,1:T(4,128)S(1)}, f32[128,4]{0,1:T(4,128)}, u32[]{:S(2)}) copy-start(f32[128,4]{0,1:T(4,128)} %param.37) | copy-start | bytes 6148
  88.6 19.3 %copy-start.46 = (f32[128]{0:T(128)}, f32[128]{0:T(128)S(1)}, u32[]{:S(2)}) copy-start(f32[128]{0:T(128)S(1)} %get-tuple-element.139) | copy-start | bytes 1540
  88.6 19.3 %copy-start.48 = (f32[128]{0:T(128)}, f32[128]{0:T(128)S(1)}, u32[]{:S(2)}) copy-start(f32[128]{0:T(128)S(1)} %get-tuple-element.141) | copy-start | bytes 1540
  94.1 9.7 %copy-start.50 = (f32[4]{0:T(128)}, f32[4]{0:T(128)S(1)}, u32[]{:S(2)}) copy-start(f32[4]{0:T(128)S(1)} %get-tuple-element.142) | copy-start | bytes 52
  94.1 9.7 %copy-start.52 = (f32[4]{0:T(128)}, f32[4]{0:T(128)S(1)}, u32[]{:S(2)}) copy-start(f32[4]{0:T(128)S(1)} %get-tuple-element.143) | copy-start | bytes 52
  105.0 3.1 %copy-start.27 = (bf16[1,2560]{1,0:T(2,128)(2,1)}, bf16[1,2560]{1,0:T(2,128)(2,1)S(1)}, u32[]{:S(2)}) copy-start(bf16[1,2560]{1,0:T(2,128)(2,1)S(1)} %subtract_multiply_fusion) | copy-start | bytes 15364
  105.1 3.1 %copy-start.24 = (bf16[1,2048,1,128]{3,1,2,0:T(8,128)(2,1)S(1)}, bf16[1,2048,1,128]{3,1,2,0:T(8,128)(2,1)}, u32[]{:S(2)}) copy-start(bf16[1,2048,1,128]{3,1,2,0:T(8,128)(2,1)} %copy-done.23) | copy-start | bytes 1572868
  108.0 7.9 %copy-start.30 = (f32[1,1024]{1,0:T(1,128)}, f32[1,1024]{1,0:T(1,128)S(1)}, u32[]{:S(2)}) copy-start(f32[1,1024]{1,0:T(1,128)S(1)} %slice.261) | copy-start | bytes 12292
  108.6 7.9 %copy-start.16 = (f32[128,512]{1,0:T(8,128)}, f32[128,512]{1,0:T(8,128)S(1)}, u32[]{:S(2)}) copy-start(f32[128,512]{1,0:T(8,128)S(1)} %fusion.60) | copy-start | bytes 786436
  112.0 2.6 %copy-start.1 = (bf16[512,2048]{1,0:T(8,128)(2,1)}, bf16[512,2048]{1,0:T(8,128)(2,1)S(1)}, u32[]{:S(2)}) copy-start(bf16[512,2048]{1,0:T(8,128)(2,1)S(1)} %fusion.22) | copy-start | bytes 6291460
  112.0 2.2 %copy-start.8 = (bf16[1,512,1536]{2,1,0:T(8,128)(2,1)S(1)}, bf16[1,512,1536]{2,1,0:T(8,128)(2,1)}, u32[]{:S(2)}) copy-start(bf16[1,512,1536]{2,1,0:T(8,128)(2,1)} %copy-done.7) | copy-start | bytes 4718596
  112.0 2.6 %copy-start.13 = (bf16[1,512,1024]{2,1,0:T(8,128)(2,1)S(1)}, bf16[1,512,1024]{2,1,0:T(8,128)(2,1)}, u32[]{:S(2)}) copy-start(bf16[1,512,1024]{2,1,0:T(8,128)(2,1)} %copy-done.12) | copy-start | bytes 3145732
  117.3 3.7 %copy-start.10 = (f32[512,4,128]{2,0,1:T(8,128)S(1)}, f32[512,4,128]{2,0,1:T(8,128)}, u32[]{:S(2)}) copy-start(f32[512,4,128]{2,0,1:T(8,128)} %copy-done.9) | copy-start | bytes 3145732
  123.9 9.2 %copy-start.6 = (f32[512,4,128]{2,0,1:T(8,128)S(1)}, f32[512,4,128]{2,0,1:T(8,128)}, u32[]{:S(2)}) copy-start(f32[512,4,128]{2,0,1:T(8,128)} %copy-done.3) | copy-start | bytes 3145732
  126.8 7.6 %copy-start.25 = (f32[512,1,128]{0,2,1:T(8,128)S(1)}, f32[512,1,128]{0,2,1:T(8,128)}, u32[]{:S(2)}) copy-start(f32[512,1,128]{0,2,1:T(8,128)} %convolution_bitcast_fusion.3) | copy-start | bytes 786436
  128.9 16.3 %all-to-all-start.3 = ((bf16[4,512,128]{1,2,0:T(8,128)(2,1)}), bf16[4,512,128]{1,2,0:T(8,128)(2,1)}, u32[]{:S(2)}, u32[]{:S(2)}) async-start(bf16[4,512,128]{1,2,0:T(8,128)(2,1)} %copy.48), calls=%async_computation.3 | async-start | bytes 1048576 | tf_op jit(solution)/shard_map/all_to_all | solution.py:230
  134.4 2.1 %copy-start.20 = (bf16[1,2048,1,128]{3,1,2,0:T(8,128)(2,1)S(1)}, bf16[1,2048,1,128]{3,1,2,0:T(8,128)(2,1)}, u32[]{:S(2)}) copy-start(bf16[1,2048,1,128]{3,1,2,0:T(8,128)(2,1)} %copy-done.19) | copy-start | bytes 1572868
  134.4 2.1 %copy-start.40 = (f32[512]{0:T(512)S(1)}, f32[512]{0:T(512)}, u32[]{:S(2)}) copy-start(f32[512]{0:T(512)} %copy-done.39) | copy-start | bytes 6148
  134.4 2.1 %copy-start.43 = (f32[512]{0:T(512)S(1)}, f32[512]{0:T(512)}, u32[]{:S(2)}) copy-start(f32[512]{0:T(512)} %get-tuple-element.150) | copy-start | bytes 6148
  136.5 1.6 copy-start.2
  136.5 1.8 %copy-start.14 = (f32[2048,1,128]{0,2,1:T(8,128)S(1)}, f32[2048,1,128]{0,2,1:T(8,128)}, u32[]{:S(2)}) copy-start(f32[2048,1,128]{0,2,1:T(8,128)} %copy.56) | copy-start | bytes 3145732
  136.5 1.8 %copy-start.34 = (f32[128]{0:T(128)S(1)}, f32[128]{0:T(128)}, u32[]{:S(2)}) copy-start(f32[128]{0:T(128)} %param.33) | copy-start | bytes 1540
  139.1 9.6 %copy-start.29 = (f32[2048]{0:T(1024)S(1)}, f32[2048]{0:T(1024)}, u32[]{:S(2)}) copy-start(f32[2048]{0:T(1024)} %get-tuple-element.167) | copy-start | bytes 24580
  139.1 9.6 %copy-start.36 = (f32[128]{0:T(128)S(1)}, f32[128]{0:T(128)}, u32[]{:S(2)}) copy-start(f32[128]{0:T(128)} %copy-done.35) | copy-start | bytes 1540
  139.5 24.9 %copy-start.38 = (bf16[128]{0:T(256)(128)(2,1)S(1)}, bf16[128]{0:T(256)(128)(2,1)}, u32[]{:S(2)}) copy-start(bf16[128]{0:T(256)(128)(2,1)} %copy-done.37) | copy-start | bytes 772
  139.5 29.9 %copy-start.28 = (bf16[1,2560]{1,0:T(2,128)(2,1)S(1)}, bf16[1,2560]{1,0:T(2,128)(2,1)}, u32[]{:S(2)}) copy-start(bf16[1,2560]{1,0:T(2,128)(2,1)} %copy-done.27) | copy-start | bytes 15364
  139.5 35.1 %copy-start.45 = (f32[128]{0:T(128)S(1)}, f32[128]{0:T(128)}, u32[]{:S(2)}) copy-start(f32[128]{0:T(128)} %get-tuple-element.137) | copy-start | bytes 1540
  139.6 35.1 %copy-start.47 = (f32[128]{0:T(128)S(1)}, f32[128]{0:T(128)}, u32[]{:S(2)}) copy-start(f32[128]{0:T(128)} %copy-done.46) | copy-start | bytes 1540
  139.6 35.1 %copy-start.49 = (f32[128]{0:T(128)S(1)}, f32[128]{0:T(128)}, u32[]{:S(2)}) copy-start(f32[128]{0:T(128)} %copy-done.48) | copy-start | bytes 1540
  139.6 35.6 %copy-start.51 = (f32[4]{0:T(128)S(1)}, f32[4]{0:T(128)}, u32[]{:S(2)}) copy-start(f32[4]{0:T(128)} %copy-done.50) | copy-start | bytes 52
  139.6 35.6 %copy-start.53 = (f32[4]{0:T(128)S(1)}, f32[4]{0:T(128)}, u32[]{:S(2)}) copy-start(f32[4]{0:T(128)} %copy-done.52) | copy-start | bytes 52
  139.6 35.6 %copy-start.54 = (f32[4]{0:T(128)S(1)}, f32[4]{0:T(128)}, u32[]{:S(2)}) copy-start(f32[4]{0:T(128)} %get-tuple-element.144) | copy-start | bytes 52
  145.2 15.7 %all-to-all-start.4 = ((bf16[4,512,128]{1,2,0:T(8,128)(2,1)}), bf16[4,512,128]{1,2,0:T(8,128)(2,1)S(1)}, u32[]{:S(2)}, u32[]{:S(2)}) async-start(bf16[4,512,128]{1,2,0:T(8,128)(2,1)} %copy.50), calls=%async_computation.4 | async-start | bytes 1048576 | tf_op jit(solution)/shard_map/all_to_all | solution.py:231
  160.9 18.9 %all-to-all-start.5 = ((bf16[4,512,128]{2,1,0:T(8,128)(2,1)}), bf16[4,512,128]{2,1,0:T(8,128)(2,1)S(1)}, u32[]{:S(2)}, u32[]{:S(2)}) async-start(bf16[4,512,128]{2,1,0:T(8,128)(2,1)} %multiply_convert_fusion), calls=%async_computation.5 | async-start | bytes 1048576 | tf_op jit(solution)/shard_map/all_to_all | solution.py:232
  (15 other events, 15.4 us)
where the time goes:
time: 182 us; the launch traced here: 181 us
  blocking collectives  46 us (25%)
  waiting for transfers between devices  40.6 us (22%)
  starting transfers between devices  25.1 us (14%)
  local copies, waits for them, and re-layouts  23 us (13%)
  other arithmetic  21.8 us (12%)
  matrix products  20.4 us (11%)
  between operations  3.64 us (2%)
    psum x1, blocking collectives, shards(): summed = lax.psum(partial_value, 'seq')  16.8 us
    all_to_all x1, waiting for transfers between devices, shards(): lax.all_to_all(widen(k_proj[0]), 'seq', split_axis=1, concat_axis=0, tile...  12.7 us
    all_to_all x1, waiting for transfers between devices, shards(): lax.all_to_all(k_terms.reshape(flat_shape), 'seq', split_axis=0, concat_a...  11.1 us
    unnamed x120, local copies, waits for them, and re-layouts  10.3 us
    all_to_all x1, waiting for transfers between devices, shards(): lax.all_to_all(q_proj[0], 'seq', split_axis=1, concat_axis=0, tiled=True)  9.79 us
    unnamed x1, blocking collectives  8.26 us
    all_to_all x1, starting transfers between devices, shards(): lax.all_to_all(widen(k_proj[0]), 'seq', split_axis=1, concat_axis=0, tile...  6.32 us
    dot_general x4, matrix products, shards(): jnp.einsum('htu,thd->uhd', grad_logits, q_block[index * block_rows:ending...  5.53 us
  transfers between devices with their start and end apart: 6, of which 5 were waited for; matrix products, arithmetic and copies ran while one was open for 15% of the time, Pallas kernels for 0%

commit v1 on v0

--- a/solution.py
+++ b/solution.py
@@ -52,7 +52,12 @@
     q_heads, k_heads, v_heads = (
         lax.all_to_all(q_proj[0], "seq", split_axis=1, concat_axis=0, tiled=True),
         lax.all_to_all(widen(k_proj[0]), "seq", split_axis=1, concat_axis=0, tiled=True),
-        lax.all_to_all(widen(v_proj[0]), "seq", split_axis=1, concat_axis=0, tiled=True),
+        jnp.concatenate(
+            lax.all_to_all(
+                jnp.stack(jnp.split(widen(v_proj[0]), lax.axis_size("seq"), axis=1)), "seq", 0, 0
+            ),
+            axis=0,
+        ),
     )
     head_shape = (passes, PASS_LEN, local_heads, HD)
     q_raw = q_heads.reshape(head_shape)

time: 182 us -> 177 us (0.973)
    unnamed x120 -> x123, local copies, waits for them, and re-layouts: 10.3 us -> 9.41 us
    another operation x4 -> x5, other arithmetic: 2.8 us -> 3.66 us
  transfers between devices with their start and end apart: 6 -> 6, of which waited for: 5 -> 5; matrix products, arithmetic and copies ran while one was open for 15% -> 16% of each run, Pallas kernels for 0% -> 0%
where the time goes in v1:
time: 177 us; the launch traced here: 176 us
  blocking collectives  46 us (26%)
  waiting for transfers between devices  39.3 us (22%)
  starting transfers between devices  24.3 us (14%)
  local copies, waits for them, and re-layouts  21.4 us (12%)
  other arithmetic  20.4 us (12%)
  matrix products  20.4 us (12%)
  between operations  3.71 us (2%)
    psum x1, blocking collectives, shards(): summed = lax.psum(partial_value, 'seq')  16.9 us
    all_to_all x1, waiting for transfers between devices, shards(): lax.all_to_all(widen(k_proj[0]), 'seq', split_axis=1, concat_axis=0, tile...  11.5 us
    all_to_all x1, waiting for transfers between devices, shards(): lax.all_to_all(k_terms.reshape(flat_shape), 'seq', split_axis=0, concat_a...  11.1 us
    all_to_all x1, waiting for transfers between devices, shards(): lax.all_to_all(q_proj[0], 'seq', split_axis=1, concat_axis=0, tiled=True)  9.79 us
    unnamed x123, local copies, waits for them, and re-layouts  9.41 us
    unnamed x1, blocking collectives  8.27 us
    all_to_all x1, starting transfers between devices, shards(): lax.all_to_all(widen(k_proj[0]), 'seq', split_axis=1, concat_axis=0, tile...  6.32 us
    dot_general x4, matrix products, shards(): jnp.einsum('htu,thd->uhd', grad_logits, q_block[index * block_rows:ending...  5.54 us
  transfers between devices with their start and end apart: 6, of which 5 were waited for; matrix products, arithmetic and copies ran while one was open for 16% of the time, Pallas kernels for 0%

profile of v1, /device:TPU:0, one launch (start us, length us, event | category | flops | bytes accessed | tf_op | source)
XLA Modules:
  0.0 175.5 jit_solution(7475644404569443490)
XLA Ops:
  0.7 1.1 copy.44
  1.8 0.8 broadcast_in_dim.27
  2.6 6.3 %all-to-all-start.1 = ((bf16[512,4,128]{0,2,1:T(8,128)(2,1)}), bf16[512,4,128]{0,2,1:T(8,128)(2,1)S(1)}, u32[]{:S(2)}, u32[]{:S(2)}) async-start(bf16[512,4,128]{0,2,1:T(8,128)(2,1)} %broadcast_in_dim.27), calls=%async_computation.1 | async-start | bytes 1048576 | tf_op jit(solution)/shard_map/all_to_all | solution.py:54
  8.9 1.0 copy.42
  11.1 0.9 pad_maximum_fusion.1
  11.9 11.5 %all-to-all-done.1 = bf16[512,4,128]{0,2,1:T(8,128)(2,1)S(1)} async-done(((bf16[512,4,128]{0,2,1:T(8,128)(2,1)}), bf16[512,4,128]{0,2,1:T(8,128)(2,1)S(1)}, u32[]{:S(2)}, u32[]{:S(2)}) %all-to-all-start.1) | async-done | bytes 524320 | tf_op jit(solution)/shard_map/all_to_all | solution.py:54
  23.4 3.5 %all-to-all-start = ((bf16[512,4,128]{0,2,1:T(8,128)(2,1)}), bf16[512,4,128]{0,2,1:T(8,128)(2,1)S(1)}, u32[]{:S(2)}, u32[]{:S(2)}) async-start(bf16[512,4,128]{0,2,1:T(8,128)(2,1)} %bitcast), calls=%async_computation | async-start | bytes 1048576 | tf_op jit(solution)/shard_map/all_to_all | solution.py:53
  31.1 9.8 %all-to-all-done = bf16[512,4,128]{0,2,1:T(8,128)(2,1)S(1)} async-done(((bf16[512,4,128]{0,2,1:T(8,128)(2,1)}), bf16[512,4,128]{0,2,1:T(8,128)(2,1)S(1)}, u32[]{:S(2)}, u32[]{:S(2)}) %all-to-all-start) | async-done | bytes 524320 | tf_op jit(solution)/shard_map/all_to_all | solution.py:53
  40.9 3.5 %all-to-all-start.2 = ((bf16[4,512,128]{2,1,0:T(8,128)(2,1)}), bf16[4,512,128]{2,1,0:T(8,128)(2,1)S(1)}, u32[]{:S(2)}, u32[]{:S(2)}) async-start(bf16[4,512,128]{2,1,0:T(8,128)(2,1)} %pad_maximum_fusion.1), calls=%async_computation.2 | async-start | bytes 1048576 | tf_op jit(solution)/shard_map/all_to_all | solution.py:56
  46.2 1.4 fusion.96
  50.7 1.0 fusion.99
  53.2 0.9 fusion.35
  54.1 1.0 fusion.16
  55.1 1.0 convert_reduce_fusion
  56.1 2.2 %all-to-all-done.2 = bf16[4,512,128]{2,1,0:T(8,128)(2,1)S(1)} async-done(((bf16[4,512,128]{2,1,0:T(8,128)(2,1)}), bf16[4,512,128]{2,1,0:T(8,128)(2,1)S(1)}, u32[]{:S(2)}, u32[]{:S(2)}) %all-to-all-start.2) | async-done | bytes 524320 | tf_op jit(solution)/shard_map/all_to_all | solution.py:56
  59.4 16.9 %psum.28 = f32[1,2560]{1,0:T(1,128)S(1)} all-reduce(f32[1,2560]{1,0:T(1,128)S(1)} %fusion.77), channel_id=1, replica_groups=mesh['grp'=2,'seq'=4,'blk'=2,'rep'=2] {'seq'}, use_global_device_ids=true, to_apply=%region_11.12 | all-reduce | flops 2560 | bytes 20480 | tf_op jit(solution)/shard_map/psum | solution.py:115
  77.6 5.2 %all-gather.1 = bf16[4,1,2560]{2,1,0:T(2,128)(2,1)S(1)} all-gather(bf16[1,1,2560]{2,1,0:T(2,128)(2,1)S(1)} %convert_bitcast_fusion.1), channel_id=1, replica_groups=mesh['grp'=2,'seq'=4,'blk'=2,'rep'=2] {'blk','rep'}, dimensions={0}, use_global_device_ids=true | all-gather | bytes 25600 | tf_op jit(solution)/shard_map/all_gather | solution.py:118
  82.8 2.0 %fusion.80 = (f32[4]{0:T(128)S(1)}, f32[128]{0:T(128)}, f32[4]{0:T(128)S(1)}, f32[128]{0:T(128)S(1)}, f32[4]{0:T(128)S(1)}, /*index=5*/f32[128]{0:T(128)S(1)}, f32[128,4]{0,1:T(4,128)S(1)}) fusion(f32[128,4]{0,1:T(4,128)S(1)} %copy-done.56, bf16[4,1,2560]{2,1,0:T(2,128)(2,1)S(1)} %all-gather.1, bf16[128,2560]{1,0:T(8,128)(2,1)} %param.36, ...), kind=kOutput, calls=%fused_computation.171 | convolution fusion | flops 3608692 | bytes 682032 | tf_op jit(solution)/shard_map/dot_general | solution.py:126
  84.8 5.4 %all-reduce.3 = (f32[4]{0:T(128)S(1)}, f32[4]{0:T(128)S(1)}, f32[4]{0:T(128)}) all-reduce(f32[4]{0:T(128)S(1)} %get-tuple-element.140, f32[4]{0:T(128)S(1)} %get-tuple-element.138, f32[4]{0:T(128)S(1)} %get-tuple-element.136), channel_id=1, replica_groups=mesh['grp'=2,'seq'=4,'blk'=2,'rep'=2] {'blk'}, use_global_device_ids=true, to_apply=%region_18.19 | all-reduce | flops 12 | bytes 96 | tf_op jit(solution)/shard_map/psum | solution.py:139
  90.2 1.4 fusion.4
  91.6 8.3 %all-reduce.2 = bf16[4,2560]{1,0:T(4,128)(2,1)S(1)} all-reduce(bf16[4,2560]{1,0:T(4,128)(2,1)S(1)} %fusion.4), channel_id=3, replica_groups=mesh['grp'=2,'seq'=4,'blk'=2,'rep'=2] {'blk'}, use_global_device_ids=true, to_apply=%region_19.20.clone | all-reduce | flops 10240 | bytes 40960
  103.6 2.1 %convolution_bitcast_fusion.3 = f32[512,1,128]{0,2,1:T(8,128)} fusion(bf16[1,2048,1,128]{3,1,2,0:T(8,128)(2,1)} %copy-done.20, bf16[1,512,512]{1,2,0:T(8,128)(2,1)S(1)} %copy-done.16, f32[512]{0:T(512)S(1)} %fusion.39, f32[512]{0:T(512)S(1)} %bitcast.275, f32[512]{0:T(512)S(1)} %get-tuple-element.152), kind=kOutput, calls=%fused_computation.63 | convolution fusion | flops 68681728 | bytes 923648 | tf_op jit(solution)/shard_map/htu,thd->uhd/dot_general | solution.py:216
  105.7 0.8 fusion.22
  107.0 1.3 fusion.87
  108.3 0.9 copy-done.8
  109.9 0.9 fusion.56
  112.2 1.1 pad_maximum_fusion
  113.4 2.5 %copy.54 = f32[2048,128]{1,0:T(8,128)} copy(f32[2048,128]{0,1:T(8,128)} %pad_maximum_fusion) | data formatting | bytes 2097152 | tf_op jit(solution)/shard_map/concatenate | solution.py:223
  115.9 1.3 copy.55
  117.2 1.6 fusion.44
  118.9 2.9 %fusion.49 = bf16[4,512,128]{2,1,0:T(8,128)(2,1)} fusion(f32[4,512,128]{2,1,0:T(8,128)} %bitcast.244, bf16[512,4,128]{2,0,1:T(8,128)(2,1)} %copy-done.14, f32[4,512]{1,0:T(4,128)S(1)} %div.160, f32[4,512]{1,0:T(4,128)} %get-tuple-element.151, f32[128]{0:T(128)} %param.32, f32[4,512]{1,0:T(4,128)} %get-tuple-element.149), kind=kLoop, calls=%fused_computation.86 | loop fusion | flops 1835008 | bytes 2122240 | tf_op jit(solution)/shard_map/convert_element_type | solution.py:28
  121.8 2.1 %copy.48 = bf16[4,512,128]{1,2,0:T(8,128)(2,1)} copy(bf16[4,512,128]{2,1,0:T(8,128)(2,1)} %fusion.49) | data formatting | bytes 1048576 | tf_op jit(solution)/shard_map/convert_element_type | solution.py:28
  123.9 4.1 %all-to-all-start.3 = ((bf16[4,512,128]{1,2,0:T(8,128)(2,1)}), bf16[4,512,128]{1,2,0:T(8,128)(2,1)}, u32[]{:S(2)}, u32[]{:S(2)}) async-start(bf16[4,512,128]{1,2,0:T(8,128)(2,1)} %copy.48), calls=%async_computation.3 | async-start | bytes 1048576 | tf_op jit(solution)/shard_map/all_to_all | solution.py:235
  128.0 1.3 copy.56
  129.5 2.0 %fusion.33 = f32[2048,1,128]{0,2,1:T(8,128)S(1)} fusion(f32[2048,1,128]{0,2,1:T(8,128)S(1)} %scatter-add.25, bf16[1,2048,1,128]{3,1,2,0:T(8,128)(2,1)} %copy-done.20, bf16[1,512,1024]{2,1,0:T(8,128)(2,1)} %copy-done.11, f32[512]{0:T(512)} %copy-done.42, f32[1024]{0:T(1024)} %bitcast.272, f32[512]{0:T(512)} %get-tuple-element.155), kind=kOutput, calls=%fused_computation.62 | convolution fusion | flops 137494528 | bytes 2236416 | tf_op jit(solution)/shard_map/htu,thd->uhd/dot_general | solution.py:216
  131.5 0.9 fusion.12
  134.6 0.9 copy.50
  135.5 4.7 %all-to-all-done.3 = bf16[4,512,128]{1,2,0:T(8,128)(2,1)} async-done(((bf16[4,512,128]{1,2,0:T(8,128)(2,1)}), bf16[4,512,128]{1,2,0:T(8,128)(2,1)}, u32[]{:S(2)}, u32[]{:S(2)}) %all-to-all-start.3) | async-done | bytes 524320 | tf_op jit(solution)/shard_map/all_to_all | solution.py:235
  140.2 3.5 %all-to-all-start.4 = ((bf16[4,512,128]{1,2,0:T(8,128)(2,1)}), bf16[4,512,128]{1,2,0:T(8,128)(2,1)S(1)}, u32[]{:S(2)}, u32[]{:S(2)}) async-start(bf16[4,512,128]{1,2,0:T(8,128)(2,1)} %copy.50), calls=%async_computation.4 | async-start | bytes 1048576 | tf_op jit(solution)/shard_map/all_to_all | solution.py:236
  143.7 1.1 multiply_convert_fusion
  144.8 11.1 %all-to-all-done.4 = bf16[4,512,128]{1,2,0:T(8,128)(2,1)S(1)} async-done(((bf16[4,512,128]{1,2,0:T(8,128)(2,1)}), bf16[4,512,128]{1,2,0:T(8,128)(2,1)S(1)}, u32[]{:S(2)}, u32[]{:S(2)}) %all-to-all-start.4) | async-done | bytes 524320 | tf_op jit(solution)/shard_map/all_to_all | solution.py:236
  155.9 3.5 %all-to-all-start.5 = ((bf16[4,512,128]{2,1,0:T(8,128)(2,1)}), bf16[4,512,128]{2,1,0:T(8,128)(2,1)S(1)}, u32[]{:S(2)}, u32[]{:S(2)}) async-start(bf16[4,512,128]{2,1,0:T(8,128)(2,1)} %multiply_convert_fusion), calls=%async_computation.5 | async-start | bytes 1048576 | tf_op jit(solution)/shard_map/all_to_all | solution.py:237
  159.4 5.0 %all-gather.2 = bf16[4,1,128]{2,1,0:T(2,128)(2,1)S(1)} all-gather(bf16[1,1,128]{2,1,0:T(2,128)(2,1)S(1)} %bitcast.278), channel_id=2, replica_groups=mesh['grp'=2,'seq'=4,'blk'=2,'rep'=2] {'blk','rep'}, dimensions={0}, use_global_device_ids=true | all-gather | bytes 1280 | tf_op jit(solution)/shard_map/all_gather | solution.py:180
  164.4 5.2 %all-gather.3 = bf16[4,1,2560]{2,1,0:T(2,128)(2,1)S(1)} all-gather(bf16[1,1,2560]{2,1,0:T(2,128)(2,1)S(1)} %bitcast.267), channel_id=1, replica_groups=mesh['grp'=2,'seq'=4,'blk'=2,'rep'=2] {'blk','rep'}, dimensions={0}, use_global_device_ids=true | all-gather | bytes 25600 | tf_op jit(solution)/shard_map/all_gather | solution.py:181
  170.7 1.2 convolution_convert_fusion
  171.9 2.0 %copy.52 = bf16[1,512,512]{2,1,0:T(8,128)(2,1)} copy(bf16[1,512,512]{1,2,0:T(8,128)(2,1)} %bitcast.66) | data formatting | bytes 1048576
  174.0 0.8 copy.53
  174.8 0.7 reduce_sum.261
  (185 shorter events, 21.2 us)
Async XLA Ops:
  0.6 58.6 %copy-start = (bf16[128,2560]{1,0:T(8,128)(2,1)S(1)}, bf16[128,2560]{1,0:T(8,128)(2,1)}, u32[]{:S(2)}) copy-start(bf16[128,2560]{1,0:T(8,128)(2,1)} %param.34) | copy-start | bytes 1966084
  0.6 8.3 %copy-start.23 = (bf16[1,512,512]{2,1,0:T(8,128)(2,1)S(1)}, bf16[1,512,512]{2,1,0:T(8,128)(2,1)}, u32[]{:S(2)}) copy-start(bf16[1,512,512]{2,1,0:T(8,128)(2,1)} %param.29) | copy-start | bytes 1572868
  0.7 9.3 %copy-start.27 = (bf16[1,512,128]{2,1,0:T(8,128)(2,1)S(1)}, bf16[1,512,128]{2,1,0:T(8,128)(2,1)}, u32[]{:S(2)}) copy-start(bf16[1,512,128]{2,1,0:T(8,128)(2,1)} %param.31) | copy-start | bytes 393220
  2.6 20.8 %all-to-all-start.1 = ((bf16[512,4,128]{0,2,1:T(8,128)(2,1)}), bf16[512,4,128]{0,2,1:T(8,128)(2,1)S(1)}, u32[]{:S(2)}, u32[]{:S(2)}) async-start(bf16[512,4,128]{0,2,1:T(8,128)(2,1)} %broadcast_in_dim.27), calls=%async_computation.1 | async-start | bytes 1048576 | tf_op jit(solution)/shard_map/all_to_all | solution.py:54
  10.1 16.9 %copy-start.57 = (u32[32]{0:T(128)S(1)}, u32[32]{0:T(128)}, u32[]{:S(2)}) copy-start(u32[32]{0:T(128)} %constant.272) | copy-start | bytes 388
  10.1 19.4 %copy-start.22 = (bf16[128,2560]{1,0:T(8,128)(2,1)S(1)}, bf16[128,2560]{1,0:T(8,128)(2,1)}, u32[]{:S(2)}) copy-start(bf16[128,2560]{1,0:T(8,128)(2,1)} %param.36) | copy-start | bytes 1966084
  23.4 17.4 %all-to-all-start = ((bf16[512,4,128]{0,2,1:T(8,128)(2,1)}), bf16[512,4,128]{0,2,1:T(8,128)(2,1)S(1)}, u32[]{:S(2)}, u32[]{:S(2)}) async-start(bf16[512,4,128]{0,2,1:T(8,128)(2,1)} %bitcast), calls=%async_computation | async-start | bytes 1048576 | tf_op jit(solution)/shard_map/all_to_all | solution.py:53
  30.7 15.5 %copy-start.3 = (f32[512,4,128]{2,0,1:T(8,128)}, f32[512,4,128]{2,0,1:T(8,128)S(1)}, u32[]{:S(2)}) copy-start(f32[512,4,128]{2,0,1:T(8,128)S(1)} %convert_element_type.401) | copy-start | bytes 3145732
  31.1 14.8 %copy-start.32 = (f32[128]{0:T(128)S(1)}, f32[128]{0:T(128)}, u32[]{:S(2)}) copy-start(f32[128]{0:T(128)} %param.32) | copy-start | bytes 1540
  40.9 17.4 %all-to-all-start.2 = ((bf16[4,512,128]{2,1,0:T(8,128)(2,1)}), bf16[4,512,128]{2,1,0:T(8,128)(2,1)S(1)}, u32[]{:S(2)}, u32[]{:S(2)}) async-start(bf16[4,512,128]{2,1,0:T(8,128)(2,1)} %pad_maximum_fusion.1), calls=%async_computation.2 | async-start | bytes 1048576 | tf_op jit(solution)/shard_map/all_to_all | solution.py:56
  44.6 3.0 %copy-start.14 = (bf16[512,4,128]{2,0,1:T(8,128)(2,1)}, bf16[512,4,128]{2,0,1:T(8,128)(2,1)S(1)}, u32[]{:S(2)}) copy-start(bf16[512,4,128]{2,0,1:T(8,128)(2,1)S(1)} %copy.43) | copy-start | bytes 1572868
  46.2 4.5 %copy-start.20 = (bf16[1,2048,1,128]{3,1,2,0:T(8,128)(2,1)}, bf16[1,2048,1,128]{3,1,2,0:T(8,128)(2,1)S(1)}, u32[]{:S(2)}) copy-start(bf16[1,2048,1,128]{3,1,2,0:T(8,128)(2,1)S(1)} %multiply_convert_fusion.2) | copy-start | bytes 1572868
  49.7 2.5 %copy-start.15 = (bf16[1,512,512]{1,2,0:T(8,128)(2,1)}, bf16[1,512,512]{1,2,0:T(8,128)(2,1)S(1)}, u32[]{:S(2)}) copy-start(bf16[1,512,512]{1,2,0:T(8,128)(2,1)S(1)} %fusion.55) | copy-start | bytes 1572868
  50.7 2.4 %copy-start.11 = (bf16[1,512,1024]{2,1,0:T(8,128)(2,1)}, bf16[1,512,1024]{2,1,0:T(8,128)(2,1)S(1)}, u32[]{:S(2)}) copy-start(bf16[1,512,1024]{2,1,0:T(8,128)(2,1)S(1)} %fusion.50) | copy-start | bytes 3145732
  52.2 1.9 %copy-start.7 = (bf16[1,512,1536]{2,1,0:T(8,128)(2,1)}, bf16[1,512,1536]{2,1,0:T(8,128)(2,1)S(1)}, u32[]{:S(2)}) copy-start(bf16[1,512,1536]{2,1,0:T(8,128)(2,1)S(1)} %fusion.27) | copy-start | bytes 4718596
  55.0 27.8 %copy-start.56 = (f32[128,4]{0,1:T(4,128)S(1)}, f32[128,4]{0,1:T(4,128)}, u32[]{:S(2)}) copy-start(f32[128,4]{0,1:T(4,128)} %param.37) | copy-start | bytes 6148
  84.8 18.1 %copy-start.47 = (f32[128]{0:T(128)}, f32[128]{0:T(128)S(1)}, u32[]{:S(2)}) copy-start(f32[128]{0:T(128)S(1)} %get-tuple-element.139) | copy-start | bytes 1540
  84.8 18.1 %copy-start.49 = (f32[128]{0:T(128)}, f32[128]{0:T(128)S(1)}, u32[]{:S(2)}) copy-start(f32[128]{0:T(128)S(1)} %get-tuple-element.141) | copy-start | bytes 1540
  90.2 9.7 %copy-start.51 = (f32[4]{0:T(128)}, f32[4]{0:T(128)S(1)}, u32[]{:S(2)}) copy-start(f32[4]{0:T(128)S(1)} %get-tuple-element.142) | copy-start | bytes 52
  90.2 9.7 %copy-start.53 = (f32[4]{0:T(128)}, f32[4]{0:T(128)S(1)}, u32[]{:S(2)}) copy-start(f32[4]{0:T(128)S(1)} %get-tuple-element.143) | copy-start | bytes 52
  99.9 3.1 %copy-start.16 = (bf16[1,512,512]{1,2,0:T(8,128)(2,1)S(1)}, bf16[1,512,512]{1,2,0:T(8,128)(2,1)}, u32[]{:S(2)}) copy-start(bf16[1,512,512]{1,2,0:T(8,128)(2,1)} %copy-done.15) | copy-start | bytes 1572868
  99.9 3.2 %copy-start.25 = (bf16[1,2048,1,128]{3,1,2,0:T(8,128)(2,1)S(1)}, bf16[1,2048,1,128]{3,1,2,0:T(8,128)(2,1)}, u32[]{:S(2)}) copy-start(bf16[1,2048,1,128]{3,1,2,0:T(8,128)(2,1)} %copy-done.24) | copy-start | bytes 1572868
  101.2 2.4 %copy-start.28 = (bf16[1,2560]{1,0:T(2,128)(2,1)}, bf16[1,2560]{1,0:T(2,128)(2,1)S(1)}, u32[]{:S(2)}) copy-start(bf16[1,2560]{1,0:T(2,128)(2,1)S(1)} %subtract_multiply_fusion) | copy-start | bytes 15364
  102.9 7.9 %copy-start.31 = (f32[1,1024]{1,0:T(1,128)}, f32[1,1024]{1,0:T(1,128)S(1)}, u32[]{:S(2)}) copy-start(f32[1,1024]{1,0:T(1,128)S(1)} %slice.261) | copy-start | bytes 12292
  103.6 7.9 %copy-start.17 = (f32[128,512]{1,0:T(8,128)}, f32[128,512]{1,0:T(8,128)S(1)}, u32[]{:S(2)}) copy-start(f32[128,512]{1,0:T(8,128)S(1)} %fusion.60) | copy-start | bytes 786436
  107.0 2.6 %copy-start.1 = (bf16[512,2048]{1,0:T(8,128)(2,1)}, bf16[512,2048]{1,0:T(8,128)(2,1)S(1)}, u32[]{:S(2)}) copy-start(bf16[512,2048]{1,0:T(8,128)(2,1)S(1)} %fusion.22) | copy-start | bytes 6291460
  107.0 2.2 %copy-start.8 = (bf16[1,512,1536]{2,1,0:T(8,128)(2,1)S(1)}, bf16[1,512,1536]{2,1,0:T(8,128)(2,1)}, u32[]{:S(2)}) copy-start(bf16[1,512,1536]{2,1,0:T(8,128)(2,1)} %copy-done.7) | copy-start | bytes 4718596
  107.0 2.6 %copy-start.12 = (bf16[1,512,1024]{2,1,0:T(8,128)(2,1)S(1)}, bf16[1,512,1024]{2,1,0:T(8,128)(2,1)}, u32[]{:S(2)}) copy-start(bf16[1,512,1024]{2,1,0:T(8,128)(2,1)} %copy-done.11) | copy-start | bytes 3145732
  112.2 3.7 %copy-start.10 = (f32[512,4,128]{2,0,1:T(8,128)S(1)}, f32[512,4,128]{2,0,1:T(8,128)}, u32[]{:S(2)}) copy-start(f32[512,4,128]{2,0,1:T(8,128)} %copy-done.9) | copy-start | bytes 3145732
  118.9 9.2 %copy-start.6 = (f32[512,4,128]{2,0,1:T(8,128)S(1)}, f32[512,4,128]{2,0,1:T(8,128)}, u32[]{:S(2)}) copy-start(f32[512,4,128]{2,0,1:T(8,128)} %copy-done.3) | copy-start | bytes 3145732
  121.8 7.6 %copy-start.26 = (f32[512,1,128]{0,2,1:T(8,128)S(1)}, f32[512,1,128]{0,2,1:T(8,128)}, u32[]{:S(2)}) copy-start(f32[512,1,128]{0,2,1:T(8,128)} %convolution_bitcast_fusion.3) | copy-start | bytes 786436
  123.9 16.3 %all-to-all-start.3 = ((bf16[4,512,128]{1,2,0:T(8,128)(2,1)}), bf16[4,512,128]{1,2,0:T(8,128)(2,1)}, u32[]{:S(2)}, u32[]{:S(2)}) async-start(bf16[4,512,128]{1,2,0:T(8,128)(2,1)} %copy.48), calls=%async_computation.3 | async-start | bytes 1048576 | tf_op jit(solution)/shard_map/all_to_all | solution.py:235
  129.3 2.1 %copy-start.21 = (bf16[1,2048,1,128]{3,1,2,0:T(8,128)(2,1)S(1)}, bf16[1,2048,1,128]{3,1,2,0:T(8,128)(2,1)}, u32[]{:S(2)}) copy-start(bf16[1,2048,1,128]{3,1,2,0:T(8,128)(2,1)} %copy-done.20) | copy-start | bytes 1572868
  129.3 2.1 %copy-start.41 = (f32[512]{0:T(512)S(1)}, f32[512]{0:T(512)}, u32[]{:S(2)}) copy-start(f32[512]{0:T(512)} %copy-done.40) | copy-start | bytes 6148
  129.3 2.1 %copy-start.44 = (f32[512]{0:T(512)S(1)}, f32[512]{0:T(512)}, u32[]{:S(2)}) copy-start(f32[512]{0:T(512)} %get-tuple-element.154) | copy-start | bytes 6148
  131.5 1.8 %copy-start.13 = (f32[2048,1,128]{0,2,1:T(8,128)S(1)}, f32[2048,1,128]{0,2,1:T(8,128)}, u32[]{:S(2)}) copy-start(f32[2048,1,128]{0,2,1:T(8,128)} %copy.56) | copy-start | bytes 3145732
  134.1 9.6 %copy-start.30 = (f32[2048]{0:T(1024)S(1)}, f32[2048]{0:T(1024)}, u32[]{:S(2)}) copy-start(f32[2048]{0:T(1024)} %get-tuple-element.171) | copy-start | bytes 24580
  134.1 9.6 %copy-start.37 = (f32[128]{0:T(128)S(1)}, f32[128]{0:T(128)}, u32[]{:S(2)}) copy-start(f32[128]{0:T(128)} %copy-done.36) | copy-start | bytes 1540
  134.5 24.9 %copy-start.39 = (bf16[128]{0:T(256)(128)(2,1)S(1)}, bf16[128]{0:T(256)(128)(2,1)}, u32[]{:S(2)}) copy-start(bf16[128]{0:T(256)(128)(2,1)} %copy-done.38) | copy-start | bytes 772
  134.5 29.9 %copy-start.29 = (bf16[1,2560]{1,0:T(2,128)(2,1)S(1)}, bf16[1,2560]{1,0:T(2,128)(2,1)}, u32[]{:S(2)}) copy-start(bf16[1,2560]{1,0:T(2,128)(2,1)} %copy-done.28) | copy-start | bytes 15364
  134.5 35.1 %copy-start.46 = (f32[128]{0:T(128)S(1)}, f32[128]{0:T(128)}, u32[]{:S(2)}) copy-start(f32[128]{0:T(128)} %get-tuple-element.137) | copy-start | bytes 1540
  134.5 35.1 %copy-start.48 = (f32[128]{0:T(128)S(1)}, f32[128]{0:T(128)}, u32[]{:S(2)}) copy-start(f32[128]{0:T(128)} %copy-done.47) | copy-start | bytes 1540
  134.5 35.1 %copy-start.50 = (f32[128]{0:T(128)S(1)}, f32[128]{0:T(128)}, u32[]{:S(2)}) copy-start(f32[128]{0:T(128)} %copy-done.49) | copy-start | bytes 1540
  134.5 35.6 %copy-start.52 = (f32[4]{0:T(128)S(1)}, f32[4]{0:T(128)}, u32[]{:S(2)}) copy-start(f32[4]{0:T(128)} %copy-done.51) | copy-start | bytes 52
  134.6 35.6 %copy-start.54 = (f32[4]{0:T(128)S(1)}, f32[4]{0:T(128)}, u32[]{:S(2)}) copy-start(f32[4]{0:T(128)} %copy-done.53) | copy-start | bytes 52
  134.6 35.6 %copy-start.55 = (f32[4]{0:T(128)S(1)}, f32[4]{0:T(128)}, u32[]{:S(2)}) copy-start(f32[4]{0:T(128)} %get-tuple-element.144) | copy-start | bytes 52
  140.2 15.7 %all-to-all-start.4 = ((bf16[4,512,128]{1,2,0:T(8,128)(2,1)}), bf16[4,512,128]{1,2,0:T(8,128)(2,1)S(1)}, u32[]{:S(2)}, u32[]{:S(2)}) async-start(bf16[4,512,128]{1,2,0:T(8,128)(2,1)} %copy.50), calls=%async_computation.4 | async-start | bytes 1048576 | tf_op jit(solution)/shard_map/all_to_all | solution.py:236
  155.9 18.9 %all-to-all-start.5 = ((bf16[4,512,128]{2,1,0:T(8,128)(2,1)}), bf16[4,512,128]{2,1,0:T(8,128)(2,1)S(1)}, u32[]{:S(2)}, u32[]{:S(2)}) async-start(bf16[4,512,128]{2,1,0:T(8,128)(2,1)} %multiply_convert_fusion), calls=%async_computation.5 | async-start | bytes 1048576 | tf_op jit(solution)/shard_map/all_to_all | solution.py:237
  (16 other events, 17.8 us)
